TPU v7x, 256 devices: a whole 4x4x8 slice. The times are simulated.
256 devices in a mesh: rep: 2 (over y_lo), seq: 64 (over x, z, core), chan: 2 (over y_hi).
Axes of the slice: x: 4, y: 4 (y_hi: 2, y_lo: 2; y = y_hi * 2 + y_lo), z: 8, core: 2. Of those that a mesh axis runs over, the one named last changes fastest.
Arguments:
- inputs: bfloat16 [2, 65536, 256], P('rep', 'seq', 'chan'), may hold values from -6 to 6
- cotangent: bfloat16 [2, 65536, 256], P('rep', 'seq', 'chan'), may hold values from -0.015625 to 0.015625
- filter_taps: bfloat16 [65536, 256], P('seq', 'chan'), may hold values from -6 to 6
- out_proj: bfloat16 [256, 256], P('chan'), may hold values from -0.375 to 0.375
Outputs:
- grad_input: bfloat16 [2, 65536, 256], P('rep', 'seq', 'chan')
- grad_filter: float32 [65536, 256], P('seq', 'chan')
All inputs are finite; a program needn't handle non-finite values.
Results may differ from a plain program's by a relative error of at most 0.0049.
Values may be sent and summed in bfloat16 or wider, within the bound.
A program may use at most 128 MiB of HBM per device.

v0:
```python
import math
import jax
import jax.numpy as jnp
from jax import lax
from jax.sharding import PartitionSpec as P

FACTOR = 16
precise_mode = lax.Precision.HIGHEST


def angle_table(numerator, modulus):
    return (numerator % modulus).astype(jnp.float32) * (2.0 * math.pi / modulus)


def dft_table(table_size, direction):
    index_row = jnp.arange(table_size, dtype=jnp.int32)
    angle_grid = angle_table(index_row[:, None] * index_row[None, :], table_size)
    return (jnp.cos(angle_grid), direction * jnp.sin(angle_grid))


def complex_apply(pattern, matrix, real_part, imag_part):
    matrix_real, matrix_imag = matrix

    def product(first_op, second_op):
        return jnp.einsum(pattern, first_op, second_op, precision=precise_mode)

    return (
        product(matrix_real, real_part) - product(matrix_imag, imag_part),
        product(matrix_real, imag_part) + product(matrix_imag, real_part),
    )


def rotate(real_part, imag_part, angle_grid, direction):
    cosine = jnp.cos(angle_grid)
    sine_part = direction * jnp.sin(angle_grid)
    return (real_part * cosine - imag_part * sine_part, real_part * sine_part + imag_part * cosine)


def twist_signal(values, positions, seq_length):
    angle_grid = angle_table(positions, 2 * seq_length)[:, :, None]
    real_part = jnp.stack([values, values * jnp.cos(angle_grid)])
    imag_part = jnp.stack([jnp.zeros_like(values), -values * jnp.sin(angle_grid)])
    return (real_part, imag_part)


def untwist(real_part, imag_part, positions, seq_length):
    angle_grid = angle_table(positions, 2 * seq_length)[:, :, None]
    running = real_part[0] + real_part[1] * jnp.cos(angle_grid) - imag_part[1] * jnp.sin(angle_grid)
    return running / (2.0 * seq_length)


def twiddle_rows(real_part, imag_part, freq_index, row_index, seq_length, direction):
    angle_grid = angle_table(freq_index[:, None] * row_index[None, :], seq_length)[None, :, :, None]
    return rotate(real_part, imag_part, angle_grid, direction)


def rows_forward(real_part, imag_part):
    twists, groups, tok_rows, part_width = real_part.shape
    outer_size = tok_rows // FACTOR
    real_part = real_part.reshape(twists, groups, outer_size, FACTOR, part_width)
    imag_part = imag_part.reshape(twists, groups, outer_size, FACTOR, part_width)
    real_part, imag_part = complex_apply(
        "qr,bkrsc->bkqsc", dft_table(outer_size, -1.0), real_part, imag_part
    )
    outer_index = jnp.arange(outer_size, dtype=jnp.int32)
    inner_index = jnp.arange(FACTOR, dtype=jnp.int32)
    angle_grid = angle_table(outer_index[:, None] * inner_index[None, :], tok_rows)[
        None, None, :, :, None
    ]
    real_part, imag_part = rotate(real_part, imag_part, angle_grid, -1.0)
    return complex_apply("ps,bkqsc->bkqpc", dft_table(FACTOR, -1.0), real_part, imag_part)


def rows_inverse(real_part, imag_part):
    twists, groups, outer_size, inner_size, part_width = real_part.shape
    tok_rows = outer_size * inner_size
    real_part, imag_part = complex_apply(
        "sp,bkqpc->bkqsc", dft_table(inner_size, 1.0), real_part, imag_part
    )
    outer_index = jnp.arange(outer_size, dtype=jnp.int32)
    inner_index = jnp.arange(inner_size, dtype=jnp.int32)
    angle_grid = angle_table(outer_index[:, None] * inner_index[None, :], tok_rows)[
        None, None, :, :, None
    ]
    real_part, imag_part = rotate(real_part, imag_part, angle_grid, 1.0)
    real_part, imag_part = complex_apply(
        "rq,bkqsc->bkrsc", dft_table(outer_size, 1.0), real_part, imag_part
    )
    return (
        real_part.reshape(twists, groups, tok_rows, part_width),
        imag_part.reshape(twists, groups, tok_rows, part_width),
    )


def conj_product(first_real, first_imag, second_real, second_imag):
    return (
        first_real * second_real + first_imag * second_imag,
        first_imag * second_real - first_real * second_imag,
    )


def per_device(inputs, cotangent, filter_taps, out_proj):
    devices = lax.axis_size("seq")
    seq_index = lax.axis_index("seq")
    tok_rows = inputs.shape[1]
    chan_width = inputs.shape[2]
    seq_length = devices * tok_rows
    grad_seq = cotangent.reshape(tok_rows, chan_width)
    projected = lax.dot_general(
        lax.all_gather(grad_seq, "chan", axis=1, tiled=True),
        out_proj,
        (((1,), (1,)), ((), ())),
        preferred_element_type=jnp.float32,
    )
    grad_mixed = projected.astype(jnp.bfloat16)
    signals = (grad_mixed, inputs.reshape(tok_rows, chan_width), filter_taps)
    device_index = jnp.arange(devices, dtype=jnp.int32)
    block_rows = tok_rows // devices
    pieces = (
        lax.all_to_all(signals[0], "seq", split_axis=0, concat_axis=0, tiled=True),
        lax.all_to_all(signals[1], "seq", split_axis=0, concat_axis=0, tiled=True),
        lax.all_to_all(signals[2], "seq", split_axis=0, concat_axis=0, tiled=True),
    )
    stacked = jnp.concatenate([member.astype(jnp.float32) for member in pieces], axis=1)
    stacked = stacked.reshape(devices, block_rows, 3 * chan_width)
    local_rows = seq_index * block_rows + jnp.arange(block_rows, dtype=jnp.int32)
    positions = device_index[:, None] * tok_rows + local_rows[None, :]
    real_part, imag_part = twist_signal(stacked, positions, seq_length)
    real_part, imag_part = complex_apply(
        "kp,bpsc->bksc", dft_table(devices, -1.0), real_part, imag_part
    )
    real_part, imag_part = twiddle_rows(
        real_part, imag_part, device_index, local_rows, seq_length, -1.0
    )
    real_part, imag_part = (
        lax.all_to_all(real_part, "seq", split_axis=1, concat_axis=2, tiled=True),
        lax.all_to_all(imag_part, "seq", split_axis=1, concat_axis=2, tiled=True),
    )
    real_part, imag_part = rows_forward(real_part, imag_part)
    part_width = real_part.shape[-1] // 3
    grad_real = real_part[..., :part_width]
    grad_imag = imag_part[..., :part_width]
    input_real = real_part[..., part_width : 2 * part_width]
    input_imag = imag_part[..., part_width : 2 * part_width]
    taps_real = real_part[..., 2 * part_width :]
    taps_imag = imag_part[..., 2 * part_width :]
    du_real, du_imag = conj_product(grad_real, grad_imag, taps_real, taps_imag)
    dk_real, dk_imag = conj_product(grad_real, grad_imag, input_real, input_imag)
    dk_real, dk_imag = lax.psum((dk_real, dk_imag), "rep")
    joined_real = jnp.concatenate([du_real, dk_real], axis=4)
    joined_imag = jnp.concatenate([du_imag, dk_imag], axis=4)
    real_part, imag_part = rows_inverse(joined_real, joined_imag)
    freq_here = jnp.reshape(seq_index, (1,))
    all_rows = jnp.arange(tok_rows, dtype=jnp.int32)
    real_part, imag_part = twiddle_rows(real_part, imag_part, freq_here, all_rows, seq_length, 1.0)
    real_part, imag_part = (
        lax.all_to_all(real_part, "seq", split_axis=2, concat_axis=1, tiled=True),
        lax.all_to_all(imag_part, "seq", split_axis=2, concat_axis=1, tiled=True),
    )
    real_part, imag_part = complex_apply(
        "pk,bksc->bpsc", dft_table(devices, 1.0), real_part, imag_part
    )
    values = untwist(real_part, imag_part, positions, seq_length)
    grad_rows = values[:, :, :part_width].astype(jnp.bfloat16).reshape(tok_rows, part_width)
    grad_input = lax.all_to_all(grad_rows, "seq", split_axis=0, concat_axis=0, tiled=True)
    filter_rows = values[:, :, part_width:].reshape(tok_rows, values.shape[2] - part_width)
    grad_filter = lax.all_to_all(filter_rows, "seq", split_axis=0, concat_axis=0, tiled=True)
    return (grad_input.reshape(1, tok_rows, chan_width), grad_filter)


def solution(mesh):
    return jax.shard_map(
        per_device,
        mesh=mesh,
        in_specs=(
            P("rep", "seq", "chan"),
            P("rep", "seq", "chan"),
            P("seq", "chan"),
            P("chan", None),
        ),
        out_specs=(P("rep", "seq", "chan"), P("seq", "chan")),
        check_vma=False,
    )
```

profile of v0, /device:TPU:1, one launch (start us, length us, event | category | flops | bytes accessed | tf_op | source)
XLA Modules:
  0.0 586.2 jit_solution(16802311897165362928)
XLA Ops:
  7.2 9.9 %all-gather = bf16[1,1024,256]{2,1,0:T(8,128)(2,1)S(1)} all-gather(bf16[1,1024,128]{2,1,0:T(8,128)(2,1)} %param.5), channel_id=2, replica_groups=mesh['rep'=2,'seq'=64,'chan'=2] {'chan'}, dimensions={2}, use_global_device_ids=true | all-gather | bytes 786432 | tf_op jit(solution)/shard_map/all_gather | solution.py:110
  17.1 0.3 convolution_convert_fusion
  17.4 25.4 %all_to_all.84 = bf16[64,16,128]{2,1,0:T(8,128)(2,1)S(1)} all-to-all(bf16[64,16,128]{2,1,0:T(8,128)(2,1)S(1)} %bitcast.244), channel_id=1, replica_groups=mesh['rep'=2,'seq'=64,'chan'=2] {'seq'}, dimensions={0} | all-to-all | bytes 524288 | tf_op jit(solution)/shard_map/all_to_all | solution.py:120
  42.9 17.8 %all_to_all.85 = bf16[64,16,128]{2,1,0:T(8,128)(2,1)S(1)} all-to-all(bf16[64,16,128]{2,1,0:T(8,128)(2,1)S(1)} %bitcast.245), channel_id=1, replica_groups=mesh['rep'=2,'seq'=64,'chan'=2] {'seq'}, dimensions={0} | all-to-all | bytes 524288 | tf_op jit(solution)/shard_map/all_to_all | solution.py:122
  60.7 6.5 %all-to-all-start.1 = ((bf16[64,16,128]{2,1,0:T(8,128)(2,1)}), bf16[64,16,128]{2,1,0:T(8,128)(2,1)S(1)}, u32[]{:S(2)}, u32[]{:S(2)}) async-start(bf16[64,16,128]{2,1,0:T(8,128)(2,1)} %bitcast.3), calls=%async_computation.1 | async-start | bytes 524288 | tf_op jit(solution)/shard_map/all_to_all | solution.py:121
  67.2 0.2 fusion.182
  67.5 11.5 %all-to-all-done.1 = bf16[64,16,128]{2,1,0:T(8,128)(2,1)S(1)} async-done(((bf16[64,16,128]{2,1,0:T(8,128)(2,1)}), bf16[64,16,128]{2,1,0:T(8,128)(2,1)S(1)}, u32[]{:S(2)}, u32[]{:S(2)}) %all-to-all-start.1) | async-done | bytes 262176 | tf_op jit(solution)/shard_map/all_to_all | solution.py:121
  79.1 0.1 fusion.296
  79.3 2.4 fusion.72
  81.6 2.4 fusion.73
  84.0 0.2 convert_multiply_fusion
  84.2 3.3 fusion.56
  87.5 17.7 %fusion.4 = (f32[2,64,16,384]{3,1,2,0:T(8,128)}, f32[2,64,16,384]{3,1,2,0:T(8,128)S(1)}) fusion(f32[2,16,384,64]{2,3,1,0:T(8,128)S(1)} %fusion.56, f32[64,16]{0,1:T(8,128)S(1)} %get-tuple-element.19, f32[64,16]{0,1:T(8,128)S(1)} %get-tuple-element.18, f32[2,16,384,64]{2,3,1,0:T(8,128)S(1)} %fusion.73, f32[1,64,16,384]{3,1,2,0:T(8,128)S(1)} %convert_multiply_fusion, ...), kind=kOutput, calls=%fused_computation.11 | convolution fusion | flops 610332672 | bytes 15736832 | tf_op jit(solution)/shard_map/kp,bpsc->bksc/dot_general | solution.py:25
  105.3 3.5 copy.43
  108.8 6.0 %all-to-all-start.4 = ((f32[2,64,16,384]{3,2,0,1:T(8,128)}), f32[2,64,16,384]{3,2,0,1:T(8,128)S(1)}, u32[]{:S(2)}, u32[]{:S(2)}) async-start(f32[2,64,16,384]{3,2,0,1:T(8,128)} %copy.43), calls=%async_computation.4 | async-start | bytes 6291456 | tf_op jit(solution)/shard_map/all_to_all | solution.py:137
  114.8 5.3 copy.41
  120.2 68.2 %all-to-all-done.4 = f32[2,64,16,384]{3,2,0,1:T(8,128)S(1)} async-done(((f32[2,64,16,384]{3,2,0,1:T(8,128)}), f32[2,64,16,384]{3,2,0,1:T(8,128)S(1)}, u32[]{:S(2)}, u32[]{:S(2)}) %all-to-all-start.4) | async-done | bytes 3145760 | tf_op jit(solution)/shard_map/all_to_all | solution.py:137
  188.4 1.7 copy-done.2
  190.1 6.1 %all-to-all-start.3 = ((f32[2,64,16,384]{3,2,0,1:T(8,128)}), f32[2,64,16,384]{3,2,0,1:T(8,128)S(1)}, u32[]{:S(2)}, u32[]{:S(2)}) async-start(f32[2,64,16,384]{3,2,0,1:T(8,128)} %copy.41), calls=%async_computation.3 | async-start | bytes 6291456 | tf_op jit(solution)/shard_map/all_to_all | solution.py:136
  196.3 8.5 %fusion.16 = f32[2,16,384,64]{2,3,1,0:T(8,128)} fusion(f32[2,64,16,384]{3,2,0,1:T(8,128)} %copy-done.2), kind=kOutput, calls=%fused_computation.27 | convolution fusion | flops 604041216 | bytes 6291456 | tf_op jit(solution)/shard_map/qr,bkrsc->bkqsc/dot_general | solution.py:25
  204.8 6.6 %fusion.14 = f32[2,16,384,64]{2,3,1,0:T(8,128)} fusion(f32[2,64,16,384]{3,2,0,1:T(8,128)S(1)} %copy-done.3), kind=kOutput, calls=%fused_computation.25 | convolution fusion | flops 604037120 | bytes 6291456 | tf_op jit(solution)/shard_map/qr,bkrsc->bkqsc/dot_general | solution.py:25
  211.4 58.2 %all-to-all-done.3 = f32[2,64,16,384]{3,2,0,1:T(8,128)S(1)} async-done(((f32[2,64,16,384]{3,2,0,1:T(8,128)}), f32[2,64,16,384]{3,2,0,1:T(8,128)S(1)}, u32[]{:S(2)}, u32[]{:S(2)}) %all-to-all-start.3) | async-done | bytes 3145760 | tf_op jit(solution)/shard_map/all_to_all | solution.py:136
  269.7 7.5 %fusion.46 = f32[2,16,384,64]{2,3,1,0:T(8,128)S(1)} fusion(f32[2,16,384,64]{2,3,1,0:T(8,128)} %fusion.16, f32[2,64,16,384]{3,2,0,1:T(8,128)S(1)} %all-to-all-done.3), kind=kOutput, calls=%fused_computation.71 | convolution fusion | flops 604823552 | bytes 9437184 | tf_op jit(solution)/shard_map/qr,bkrsc->bkqsc/dot_general | solution.py:25
  277.2 6.2 %fusion.1 = (f32[2,64,16,384]{3,1,2,0:T(8,128)S(1)}, f32[2,64,16,384]{3,1,2,0:T(8,128)S(1)}) fusion(f32[2,16,384,64]{2,3,1,0:T(8,128)S(1)} %fusion.46, f32[64,16]{0,1:T(8,128)S(1)} %get-tuple-element.24, f32[64,16]{0,1:T(8,128)S(1)} %get-tuple-element.25, f32[2,16,384,64]{2,3,1,0:T(8,128)S(1)} %copy-done.4, f32[2,64,16,384]{3,2,0,1:T(8,128)S(1)} %all-to-all-done.3), kind=kOutput, calls=%fused_computation.4 | convolution fusion | flops 609546240 | bytes 15736832 | tf_op jit(solution)/shard_map/qr,bkrsc->bkqsc/dot_general | solution.py:25
  283.4 4.8 fusion.8
  288.3 4.7 fusion.6
  293.0 4.8 subtract_bitcast_fusion
  297.8 5.0 add_bitcast_fusion
  302.8 1.8 multiply_add_fusion.1
  304.6 0.1 copy.51
  304.9 71.6 %all-reduce.4.cloned.1.call-done = (f32[2,1,64,16,128]{4,3,2,0,1:T(8,128)}, f32[2,1,64,16,128]{4,3,2,0,1:T(8,128)}) async-done(((f32[2,1,64,16,128]{4,3,2,0,1:T(8,128)}, f32[2,1,64,16,128]{4,3,2,0,1:T(8,128)}), (f32[2,1,64,16,128]{4,3,2,0,1:T(8,128)}, f32[2,1,64,16,128]{4,3,2,0,1:T(8,128)})) %all-reduce.4.cloned.1.call-update) | async-done | bytes 2097168 | tf_op jit(solution)/shard_map/psum | solution.py:149
  376.5 3.3 fusion.58
  379.8 2.0 fusion.59
  381.8 2.1 fusion.62
  383.9 3.0 fusion.27
  387.0 3.4 fusion.40
  390.4 3.3 fusion.38
  393.7 3.5 subtract_bitcast_fusion.2
  397.2 1.2 copy.55
  398.4 3.6 add_bitcast_fusion.2
  402.0 1.2 copy.58
  403.2 0.5 fusion.24
  403.7 2.9 copy.62
  406.7 10.9 %all-to-all-start.6 = ((f32[2,1,1024,256]{3,0,1,2:T(2,128)}), f32[2,1,1024,256]{3,0,1,2:T(2,128)}, u32[]{:S(2)}, u32[]{:S(2)}) async-start(f32[2,1,1024,256]{3,0,1,2:T(2,128)} %copy.62), calls=%async_computation.6 | async-start | bytes 4194304 | tf_op jit(solution)/shard_map/all_to_all | solution.py:158
  417.5 3.0 copy.59
  420.5 48.2 %all-to-all-done.6 = f32[2,1,1024,256]{3,0,1,2:T(2,128)} async-done(((f32[2,1,1024,256]{3,0,1,2:T(2,128)}), f32[2,1,1024,256]{3,0,1,2:T(2,128)}, u32[]{:S(2)}, u32[]{:S(2)}) %all-to-all-start.6) | async-done | bytes 2097184 | tf_op jit(solution)/shard_map/all_to_all | solution.py:158
  468.7 6.2 %all-to-all-start.5 = ((f32[2,1,1024,256]{3,0,1,2:T(2,128)}), f32[2,1,1024,256]{3,0,1,2:T(2,128)}, u32[]{:S(2)}, u32[]{:S(2)}) async-start(f32[2,1,1024,256]{3,0,1,2:T(2,128)} %copy.59), calls=%async_computation.5 | async-start | bytes 4194304 | tf_op jit(solution)/shard_map/all_to_all | solution.py:157
  474.9 1.8 copy.63
  476.7 4.7 fusion.32
  481.4 3.3 fusion.30
  484.7 41.2 %all-to-all-done.5 = f32[2,1,1024,256]{3,0,1,2:T(2,128)} async-done(((f32[2,1,1024,256]{3,0,1,2:T(2,128)}), f32[2,1,1024,256]{3,0,1,2:T(2,128)}, u32[]{:S(2)}, u32[]{:S(2)}) %all-to-all-start.5) | async-done | bytes 2097184 | tf_op jit(solution)/shard_map/all_to_all | solution.py:157
  525.9 1.9 copy.60
  527.8 0.3 copy-done.5
  528.1 3.3 subtract_bitcast_fusion.1
  531.4 3.6 add_bitcast_fusion.1
  535.1 0.4 fusion.78
  535.5 0.9 copy.67
  536.4 5.8 all-to-all-start.7
  542.2 1.1 copy.68
  543.3 10.8 %all-to-all-done.7 = bf16[64,16,128]{2,1,0:T(8,128)(2,1)S(1)} async-done(((bf16[64,16,128]{2,1,0:T(8,128)(2,1)}), bf16[64,16,128]{2,1,0:T(8,128)(2,1)S(1)}, u32[]{:S(2)}, u32[]{:S(2)}) %all-to-all-start.7) | async-done | bytes 262176 | tf_op jit(solution)/shard_map/all_to_all | solution.py:165
  554.2 6.0 %all-to-all-start.8 = ((f32[64,16,128]{2,1,0:T(8,128)}), f32[64,16,128]{2,1,0:T(8,128)S(1)}, u32[]{:S(2)}, u32[]{:S(2)}) async-start(f32[64,16,128]{2,1,0:T(8,128)} %copy.68), calls=%async_computation.8 | async-start | bytes 1048576 | tf_op jit(solution)/shard_map/all_to_all | solution.py:167
  560.2 17.3 %all-to-all-done.8 = f32[64,16,128]{2,1,0:T(8,128)S(1)} async-done(((f32[64,16,128]{2,1,0:T(8,128)}), f32[64,16,128]{2,1,0:T(8,128)S(1)}, u32[]{:S(2)}, u32[]{:S(2)}) %all-to-all-start.8) | async-done | bytes 524320 | tf_op jit(solution)/shard_map/all_to_all | solution.py:167
  577.5 0.7 copy.135
  578.3 0.8 copy.136
  (29 shorter events, 0.6 us)
Async XLA Ops:
  7.2 10.0 %copy-start = (bf16[128,256]{1,0:T(8,128)(2,1)S(1)}, bf16[128,256]{1,0:T(8,128)(2,1)}, u32[]{:S(2)}) copy-start(bf16[128,256]{1,0:T(8,128)(2,1)} %param.7) | copy-start | bytes 196612
  7.2 35.7 %copy-start.8 = (bf16[1024,128]{1,0:T(8,128)(2,1)S(1)}, bf16[1024,128]{1,0:T(8,128)(2,1)}, u32[]{:S(2)}) copy-start(bf16[1024,128]{1,0:T(8,128)(2,1)} %param.6) | copy-start | bytes 786436
  60.7 18.4 %all-to-all-start.1 = ((bf16[64,16,128]{2,1,0:T(8,128)(2,1)}), bf16[64,16,128]{2,1,0:T(8,128)(2,1)S(1)}, u32[]{:S(2)}, u32[]{:S(2)}) async-start(bf16[64,16,128]{2,1,0:T(8,128)(2,1)} %bitcast.3), calls=%async_computation.1 | async-start | bytes 524288 | tf_op jit(solution)/shard_map/all_to_all | solution.py:121
  108.8 79.5 %all-to-all-start.4 = ((f32[2,64,16,384]{3,2,0,1:T(8,128)}), f32[2,64,16,384]{3,2,0,1:T(8,128)S(1)}, u32[]{:S(2)}, u32[]{:S(2)}) async-start(f32[2,64,16,384]{3,2,0,1:T(8,128)} %copy.43), calls=%async_computation.4 | async-start | bytes 6291456 | tf_op jit(solution)/shard_map/all_to_all | solution.py:137
  188.3 1.7 copy-start.2
  190.1 79.6 %all-to-all-start.3 = ((f32[2,64,16,384]{3,2,0,1:T(8,128)}), f32[2,64,16,384]{3,2,0,1:T(8,128)S(1)}, u32[]{:S(2)}, u32[]{:S(2)}) async-start(f32[2,64,16,384]{3,2,0,1:T(8,128)} %copy.41), calls=%async_computation.3 | async-start | bytes 6291456 | tf_op jit(solution)/shard_map/all_to_all | solution.py:136
  196.2 180.4 %all-reduce.4.cloned.1.call-start = ((), (), s32[]{:S(2)}) async-start(), calls=%async_computation.9 | async-start | bytes 4194304 | tf_op jit(solution)/shard_map/psum | solution.py:149
  196.3 8.5 %copy-start.3 = (f32[2,64,16,384]{3,2,0,1:T(8,128)S(1)}, f32[2,64,16,384]{3,2,0,1:T(8,128)}, u32[]{:S(2)}) copy-start(f32[2,64,16,384]{3,2,0,1:T(8,128)} %copy-done.2) | copy-start | bytes 9437188
  269.7 7.5 %copy-start.4 = (f32[2,16,384,64]{2,3,1,0:T(8,128)S(1)}, f32[2,16,384,64]{2,3,1,0:T(8,128)}, u32[]{:S(2)}) copy-start(f32[2,16,384,64]{2,3,1,0:T(8,128)} %fusion.14) | copy-start | bytes 9437188
  376.5 3.3 copy-start.7
  379.8 2.0 copy-start.6
  406.7 62.0 %all-to-all-start.6 = ((f32[2,1,1024,256]{3,0,1,2:T(2,128)}), f32[2,1,1024,256]{3,0,1,2:T(2,128)}, u32[]{:S(2)}, u32[]{:S(2)}) async-start(f32[2,1,1024,256]{3,0,1,2:T(2,128)} %copy.62), calls=%async_computation.6 | async-start | bytes 4194304 | tf_op jit(solution)/shard_map/all_to_all | solution.py:158
  468.7 57.2 %all-to-all-start.5 = ((f32[2,1,1024,256]{3,0,1,2:T(2,128)}), f32[2,1,1024,256]{3,0,1,2:T(2,128)}, u32[]{:S(2)}, u32[]{:S(2)}) async-start(f32[2,1,1024,256]{3,0,1,2:T(2,128)} %copy.59), calls=%async_computation.5 | async-start | bytes 4194304 | tf_op jit(solution)/shard_map/all_to_all | solution.py:157
  525.9 2.2 copy-start.5
  536.4 17.8 %all-to-all-start.7 = ((bf16[64,16,128]{2,1,0:T(8,128)(2,1)}), bf16[64,16,128]{2,1,0:T(8,128)(2,1)S(1)}, u32[]{:S(2)}, u32[]{:S(2)}) async-start(bf16[64,16,128]{2,1,0:T(8,128)(2,1)} %copy.67), calls=%async_computation.7 | async-start | bytes 524288 | tf_op jit(solution)/shard_map/all_to_all | solution.py:165
  542.2 36.9 %copy-start.1 = (bf16[128,256]{1,0:T(8,128)(2,1)S(1)}, bf16[128,256]{1,0:T(8,128)(2,1)}, u32[]{:S(2)}) copy-start(bf16[128,256]{1,0:T(8,128)(2,1)} %param.7) | copy-start | bytes 196612
  554.2 23.4 %all-to-all-start.8 = ((f32[64,16,128]{2,1,0:T(8,128)}), f32[64,16,128]{2,1,0:T(8,128)S(1)}, u32[]{:S(2)}, u32[]{:S(2)}) async-start(f32[64,16,128]{2,1,0:T(8,128)} %copy.68), calls=%async_computation.8 | async-start | bytes 1048576 | tf_op jit(solution)/shard_map/all_to_all | solution.py:167
Sparse Core Ops, SparseCore 0:
  304.7 71.7 all-reduce.3
where the time goes:
time: 590 us; the launch traced here: 586 us
  waiting for transfers between devices  327 us (55%)
  matrix products  113 us (19%)
  blocking collectives  53.2 us (9%)
  starting transfers between devices  47.6 us (8%)
  local copies, waits for them, and re-layouts  26.9 us (5%)
  between operations  14.7 us (2%)
    dot_general x24, matrix products, product(): return jnp.einsum(pattern, first_op, second_op, precision=precise_mode)  113 us
    psum x1, waiting for transfers between devices, per_device(): dk_real, dk_imag = lax.psum((dk_real, dk_imag), 'rep')  71.6 us
    all_to_all x1, waiting for transfers between devices, per_device(): lax.all_to_all(imag_part, 'seq', split_axis=1, concat_axis=2, tiled=True)  68.2 us
    all_to_all x1, waiting for transfers between devices, per_device(): lax.all_to_all(real_part, 'seq', split_axis=1, concat_axis=2, tiled=True)  58.2 us
    all_to_all x1, waiting for transfers between devices, per_device(): lax.all_to_all(imag_part, 'seq', split_axis=2, concat_axis=1, tiled=True)  48.2 us
    all_to_all x1, waiting for transfers between devices, per_device(): lax.all_to_all(real_part, 'seq', split_axis=2, concat_axis=1, tiled=True)  41.2 us
    all_to_all x1, blocking collectives, per_device(): lax.all_to_all(signals[0], 'seq', split_axis=0, concat_axis=0, tiled=True)  25.4 us
    all_to_all x1, blocking collectives, per_device(): lax.all_to_all(signals[2], 'seq', split_axis=0, concat_axis=0, tiled=True)  17.8 us
  transfers between devices with their start and end apart: 8, of which 8 were waited for; matrix products, arithmetic and copies ran while one was open for 6% of the time, Pallas kernels for 0%

commit v1 on v0

--- a/solution.py
+++ b/solution.py
@@ -6,6 +6,12 @@
 
 FACTOR = 16
 precise_mode = lax.Precision.HIGHEST
+
+
+def swap_blocks(x, name, split, join):
+    shards = jnp.split(x, lax.axis_size(name), axis=split)
+    arrived = lax.all_to_all(jnp.stack(shards), name, 0, 0)
+    return jnp.concatenate(arrived, axis=join)
 
 
 def angle_table(numerator, modulus):
@@ -134,7 +140,7 @@
     )
     real_part, imag_part = (
         lax.all_to_all(real_part, "seq", split_axis=1, concat_axis=2, tiled=True),
-        lax.all_to_all(imag_part, "seq", split_axis=1, concat_axis=2, tiled=True),
+        swap_blocks(imag_part, "seq", 1, 2),
     )
     real_part, imag_part = rows_forward(real_part, imag_part)
     part_width = real_part.shape[-1] // 3

time: 590 us -> 617 us (1.046)
  local copies, waits for them, and re-layouts: 26.9 us -> 63.8 us
  matrix products: 113 us -> 101 us
    unnamed x20 -> x77, local copies, waits for them, and re-layouts: 3.56 us -> 43.4 us
    dot_general x24, matrix products: 113 us -> 100 us  [product(): return jnp.einsum(pattern, first_op, second_op, precision=precise_mode)]
  transfers between devices with their start and end apart: 8 -> 8, of which waited for: 8 -> 8; matrix products, arithmetic and copies ran while one was open for 6% -> 5% of each run, Pallas kernels for 0% -> 0%
where the time goes in v1:
time: 617 us; the launch traced here: 613 us
  waiting for transfers between devices  329 us (53%)
  matrix products  101 us (16%)
  local copies, waits for them, and re-layouts  63.8 us (10%)
  blocking collectives  53.4 us (9%)
  starting transfers between devices  48.3 us (8%)
  between operations  14.7 us (2%)
    dot_general x24, matrix products, product(): return jnp.einsum(pattern, first_op, second_op, precision=precise_mode)  100 us
    psum x1, waiting for transfers between devices, per_device(): dk_real, dk_imag = lax.psum((dk_real, dk_imag), 'rep')  71.6 us
    all_to_all x1, waiting for transfers between devices, swap_blocks(): arrived = lax.all_to_all(jnp.stack(shards), name, 0, 0)  68.1 us
    all_to_all x1, waiting for transfers between devices, per_device(): lax.all_to_all(real_part, 'seq', split_axis=1, concat_axis=2, tiled=True)  59.8 us
    all_to_all x1, waiting for transfers between devices, per_device(): lax.all_to_all(imag_part, 'seq', split_axis=2, concat_axis=1, tiled=True)  48.2 us
    unnamed x77, local copies, waits for them, and re-layouts  43.4 us
    all_to_all x1, waiting for transfers between devices, per_device(): lax.all_to_all(real_part, 'seq', split_axis=2, concat_axis=1, tiled=True)  41.2 us
    all_to_all x1, blocking collectives, per_device(): lax.all_to_all(signals[0], 'seq', split_axis=0, concat_axis=0, tiled=True)  25.4 us
  transfers between devices with their start and end apart: 8, of which 8 were waited for; matrix products, arithmetic and copies ran while one was open for 5% of the time, Pallas kernels for 0%

profile of v1, /device:TPU:1, one launch (start us, length us, event | category | flops | bytes accessed | tf_op | source)
XLA Modules:
  0.0 612.7 jit_solution(4259107944136770866)
XLA Ops:
  7.2 9.9 %all-gather = bf16[1,1024,256]{2,1,0:T(8,128)(2,1)S(1)} all-gather(bf16[1,1024,128]{2,1,0:T(8,128)(2,1)} %param.5), channel_id=2, replica_groups=mesh['rep'=2,'seq'=64,'chan'=2] {'chan'}, dimensions={2}, use_global_device_ids=true | all-gather | bytes 786432 | tf_op jit(solution)/shard_map/all_gather | solution.py:116
  17.4 25.4 %all_to_all.80 = bf16[64,16,128]{2,1,0:T(8,128)(2,1)S(1)} all-to-all(bf16[64,16,128]{2,1,0:T(8,128)(2,1)S(1)} %bitcast.508), channel_id=1, replica_groups=mesh['rep'=2,'seq'=64,'chan'=2] {'seq'}, dimensions={0} | all-to-all | bytes 524288 | tf_op jit(solution)/shard_map/all_to_all | solution.py:126
  42.9 18.0 %all_to_all.81 = bf16[64,16,128]{2,1,0:T(8,128)(2,1)S(1)} all-to-all(bf16[64,16,128]{2,1,0:T(8,128)(2,1)} %bitcast.509), channel_id=1, replica_groups=mesh['rep'=2,'seq'=64,'chan'=2] {'seq'}, dimensions={0} | all-to-all | bytes 524288 | tf_op jit(solution)/shard_map/all_to_all | solution.py:128
  60.9 6.7 %all-to-all-start.1 = ((bf16[64,16,128]{2,1,0:T(8,128)(2,1)}), bf16[64,16,128]{2,1,0:T(8,128)(2,1)S(1)}, u32[]{:S(2)}, u32[]{:S(2)}) async-start(bf16[64,16,128]{2,1,0:T(8,128)(2,1)} %bitcast.510), calls=%async_computation.1 | async-start | bytes 524288 | tf_op jit(solution)/shard_map/all_to_all | solution.py:127
  67.9 11.5 %all-to-all-done.1 = bf16[64,16,128]{2,1,0:T(8,128)(2,1)S(1)} async-done(((bf16[64,16,128]{2,1,0:T(8,128)(2,1)}), bf16[64,16,128]{2,1,0:T(8,128)(2,1)S(1)}, u32[]{:S(2)}, u32[]{:S(2)}) %all-to-all-start.1) | async-done | bytes 262176 | tf_op jit(solution)/shard_map/all_to_all | solution.py:127
  79.6 2.4 fusion.74
  82.0 2.4 fusion.75
  84.6 3.4 fusion.58
  88.0 5.7 fusion.8
  97.0 0.7 constant_dynamic-update-slice_fusion.58
  100.3 0.7 constant_dynamic-update-slice_fusion.53
  110.8 0.7 constant_dynamic-update-slice_fusion.37
  111.5 0.7 constant_dynamic-update-slice_fusion.36
  112.8 0.7 constant_dynamic-update-slice_fusion.34
  114.2 0.7 constant_dynamic-update-slice_fusion.32
  115.5 0.7 constant_dynamic-update-slice_fusion.30
  118.1 0.7 constant_dynamic-update-slice_fusion.26
  123.4 0.7 constant_dynamic-update-slice_fusion.18
  132.7 0.7 constant_dynamic-update-slice_fusion.4
  136.0 6.0 all-to-all-start.4
  142.0 5.4 copy.45
  147.4 68.1 %all-to-all-done.4 = f32[64,2,1,16,384]{4,2,3,1,0:T(1,128)S(1)} async-done(((f32[64,2,1,16,384]{4,2,3,1,0:T(1,128)}), f32[64,2,1,16,384]{4,2,3,1,0:T(1,128)S(1)}, u32[]{:S(2)}, u32[]{:S(2)}) %all-to-all-start.4) | async-done | bytes 3145760 | tf_op jit(solution)/shard_map/all_to_all | solution.py:13
  215.5 6.2 %all-to-all-start.3 = ((f32[2,64,16,384]{3,2,0,1:T(8,128)}), f32[2,64,16,384]{3,2,0,1:T(8,128)}, u32[]{:S(2)}, u32[]{:S(2)}) async-start(f32[2,64,16,384]{3,2,0,1:T(8,128)} %copy.45), calls=%async_computation.3 | async-start | bytes 6291456 | tf_op jit(solution)/shard_map/all_to_all | solution.py:142
  222.3 6.6 %fusion.2 = f32[2,16,384,64]{2,3,1,0:T(8,128)} fusion(f32[2,1,64,16,384]{4,1,3,0,2:T(1,128)S(1)} %bitcast.488), kind=kOutput, calls=%fused_computation.3 | convolution fusion | flops 604041216 | bytes 6291456 | tf_op jit(solution)/shard_map/qr,bkrsc->bkqsc/dot_general | solution.py:31
  228.9 6.6 %fusion = f32[2,16,384,64]{2,3,1,0:T(8,128)} fusion(f32[2,1,64,16,384]{4,1,3,0,2:T(1,128)S(1)} %bitcast.489), kind=kOutput, calls=%fused_computation.1 | convolution fusion | flops 604037120 | bytes 6291456 | tf_op jit(solution)/shard_map/qr,bkrsc->bkqsc/dot_general | solution.py:31
  235.4 59.8 %all-to-all-done.3 = f32[2,64,16,384]{3,2,0,1:T(8,128)} async-done(((f32[2,64,16,384]{3,2,0,1:T(8,128)}), f32[2,64,16,384]{3,2,0,1:T(8,128)}, u32[]{:S(2)}, u32[]{:S(2)}) %all-to-all-start.3) | async-done | bytes 3145760 | tf_op jit(solution)/shard_map/all_to_all | solution.py:142
  295.2 8.0 %fusion.48 = f32[2,16,384,64]{2,3,1,0:T(8,128)S(1)} fusion(f32[2,16,384,64]{2,3,1,0:T(8,128)} %fusion.2, f32[2,64,16,384]{3,2,0,1:T(8,128)} %all-to-all-done.3), kind=kOutput, calls=%fused_computation.73 | convolution fusion | flops 604823552 | bytes 9437184 | tf_op jit(solution)/shard_map/qr,bkrsc->bkqsc/dot_general | solution.py:31
  303.2 6.9 %fusion.5 = (f32[2,64,16,384]{3,1,2,0:T(8,128)S(1)}, f32[2,64,16,384]{3,1,2,0:T(8,128)S(1)}) fusion(f32[2,16,384,64]{2,3,1,0:T(8,128)S(1)} %fusion.48, f32[64,16]{0,1:T(8,128)S(1)} %get-tuple-element.24, f32[64,16]{0,1:T(8,128)S(1)} %get-tuple-element.25, f32[2,16,384,64]{2,3,1,0:T(8,128)S(1)} %copy-done.2, f32[2,64,16,384]{3,2,0,1:T(8,128)} %all-to-all-done.3), kind=kOutput, calls=%fused_computation.8 | convolution fusion | flops 609546240 | bytes 15736832 | tf_op jit(solution)/shard_map/qr,bkrsc->bkqsc/dot_general | solution.py:31
  310.1 4.7 fusion.14
  314.7 4.7 fusion.12
  319.4 5.2 subtract_bitcast_fusion
  324.7 4.8 add_bitcast_fusion
  329.5 1.7 multiply_add_fusion.1
  331.5 71.6 %all-reduce.4.cloned.1.call-done = (f32[2,1,64,16,128]{4,3,2,0,1:T(8,128)}, f32[2,1,64,16,128]{4,3,2,0,1:T(8,128)}) async-done(((f32[2,1,64,16,128]{4,3,2,0,1:T(8,128)}, f32[2,1,64,16,128]{4,3,2,0,1:T(8,128)}), (f32[2,1,64,16,128]{4,3,2,0,1:T(8,128)}, f32[2,1,64,16,128]{4,3,2,0,1:T(8,128)})) %all-reduce.4.cloned.1.call-update) | async-done | bytes 2097168 | tf_op jit(solution)/shard_map/psum | solution.py:155
  403.2 3.3 fusion.60
  406.5 2.0 fusion.61
  408.5 2.3 fusion.64
  410.8 2.6 fusion.29
  413.4 3.4 fusion.42
  416.8 3.3 fusion.40
  420.1 3.7 subtract_bitcast_fusion.2
  423.8 1.2 copy.58
  425.1 3.5 add_bitcast_fusion.2
  428.6 1.2 copy.61
  430.3 2.9 copy.65
  433.3 10.8 %all-to-all-start.6 = ((f32[2,1,1024,256]{3,0,1,2:T(2,128)}), f32[2,1,1024,256]{3,0,1,2:T(2,128)}, u32[]{:S(2)}, u32[]{:S(2)}) async-start(f32[2,1,1024,256]{3,0,1,2:T(2,128)} %copy.65), calls=%async_computation.6 | async-start | bytes 4194304 | tf_op jit(solution)/shard_map/all_to_all | solution.py:164
  444.1 3.0 copy.62
  447.1 48.2 %all-to-all-done.6 = f32[2,1,1024,256]{3,0,1,2:T(2,128)} async-done(((f32[2,1,1024,256]{3,0,1,2:T(2,128)}), f32[2,1,1024,256]{3,0,1,2:T(2,128)}, u32[]{:S(2)}, u32[]{:S(2)}) %all-to-all-start.6) | async-done | bytes 2097184 | tf_op jit(solution)/shard_map/all_to_all | solution.py:164
  495.3 6.2 %all-to-all-start.5 = ((f32[2,1,1024,256]{3,0,1,2:T(2,128)}), f32[2,1,1024,256]{3,0,1,2:T(2,128)}, u32[]{:S(2)}, u32[]{:S(2)}) async-start(f32[2,1,1024,256]{3,0,1,2:T(2,128)} %copy.62), calls=%async_computation.5 | async-start | bytes 4194304 | tf_op jit(solution)/shard_map/all_to_all | solution.py:163
  501.5 1.8 copy.66
  503.2 4.7 fusion.34
  507.9 3.3 fusion.32
  511.2 41.2 %all-to-all-done.5 = f32[2,1,1024,256]{3,0,1,2:T(2,128)} async-done(((f32[2,1,1024,256]{3,0,1,2:T(2,128)}), f32[2,1,1024,256]{3,0,1,2:T(2,128)}, u32[]{:S(2)}, u32[]{:S(2)}) %all-to-all-start.5) | async-done | bytes 2097184 | tf_op jit(solution)/shard_map/all_to_all | solution.py:163
  552.5 1.9 copy.63
  554.7 3.3 subtract_bitcast_fusion.1
  558.0 3.6 add_bitcast_fusion.1
  562.0 0.9 copy.70
  562.9 5.8 all-to-all-start.7
  568.8 1.1 copy.71
  569.9 10.9 %all-to-all-done.7 = bf16[64,16,128]{2,1,0:T(8,128)(2,1)S(1)} async-done(((bf16[64,16,128]{2,1,0:T(8,128)(2,1)}), bf16[64,16,128]{2,1,0:T(8,128)(2,1)S(1)}, u32[]{:S(2)}, u32[]{:S(2)}) %all-to-all-start.7) | async-done | bytes 262176 | tf_op jit(solution)/shard_map/all_to_all | solution.py:171
  580.7 6.0 all-to-all-start.8
  586.8 17.3 %all-to-all-done.8 = f32[64,16,128]{2,1,0:T(8,128)S(1)} async-done(((f32[64,16,128]{2,1,0:T(8,128)}), f32[64,16,128]{2,1,0:T(8,128)S(1)}, u32[]{:S(2)}, u32[]{:S(2)}) %all-to-all-start.8) | async-done | bytes 524320 | tf_op jit(solution)/shard_map/all_to_all | solution.py:173
  604.1 0.7 copy.206
  604.8 0.8 copy.207
  (86 shorter events, 38.6 us)
Async XLA Ops:
  7.2 10.0 %copy-start = (bf16[128,256]{1,0:T(8,128)(2,1)S(1)}, bf16[128,256]{1,0:T(8,128)(2,1)}, u32[]{:S(2)}) copy-start(bf16[128,256]{1,0:T(8,128)(2,1)} %param.7) | copy-start | bytes 196612
  60.9 18.5 %all-to-all-start.1 = ((bf16[64,16,128]{2,1,0:T(8,128)(2,1)}), bf16[64,16,128]{2,1,0:T(8,128)(2,1)S(1)}, u32[]{:S(2)}, u32[]{:S(2)}) async-start(bf16[64,16,128]{2,1,0:T(8,128)(2,1)} %bitcast.510), calls=%async_computation.1 | async-start | bytes 524288 | tf_op jit(solution)/shard_map/all_to_all | solution.py:127
  136.0 79.5 %all-to-all-start.4 = ((f32[64,2,1,16,384]{4,2,3,1,0:T(1,128)}), f32[64,2,1,16,384]{4,2,3,1,0:T(1,128)S(1)}, u32[]{:S(2)}, u32[]{:S(2)}) async-start(f32[64,2,1,16,384]{4,2,3,1,0:T(1,128)} %constant_dynamic-update-slice_fusion), calls=%async_computation.4 | async-start | bytes 6291456 | tf_op jit(solution)/shard_map/all_to_all | solution.py:13
  215.5 79.7 %all-to-all-start.3 = ((f32[2,64,16,384]{3,2,0,1:T(8,128)}), f32[2,64,16,384]{3,2,0,1:T(8,128)}, u32[]{:S(2)}, u32[]{:S(2)}) async-start(f32[2,64,16,384]{3,2,0,1:T(8,128)} %copy.45), calls=%async_computation.3 | async-start | bytes 6291456 | tf_op jit(solution)/shard_map/all_to_all | solution.py:142
  221.8 181.4 %all-reduce.4.cloned.1.call-start = ((), (), s32[]{:S(2)}) async-start(), calls=%async_computation.9 | async-start | bytes 4194304 | tf_op jit(solution)/shard_map/psum | solution.py:155
  235.4 67.7 %copy-start.2 = (f32[2,16,384,64]{2,3,1,0:T(8,128)S(1)}, f32[2,16,384,64]{2,3,1,0:T(8,128)}, u32[]{:S(2)}) copy-start(f32[2,16,384,64]{2,3,1,0:T(8,128)} %fusion) | copy-start | bytes 9437188
  403.2 3.3 copy-start.5
  406.5 2.0 copy-start.4
  433.3 62.0 %all-to-all-start.6 = ((f32[2,1,1024,256]{3,0,1,2:T(2,128)}), f32[2,1,1024,256]{3,0,1,2:T(2,128)}, u32[]{:S(2)}, u32[]{:S(2)}) async-start(f32[2,1,1024,256]{3,0,1,2:T(2,128)} %copy.65), calls=%async_computation.6 | async-start | bytes 4194304 | tf_op jit(solution)/shard_map/all_to_all | solution.py:164
  495.3 57.2 %all-to-all-start.5 = ((f32[2,1,1024,256]{3,0,1,2:T(2,128)}), f32[2,1,1024,256]{3,0,1,2:T(2,128)}, u32[]{:S(2)}, u32[]{:S(2)}) async-start(f32[2,1,1024,256]{3,0,1,2:T(2,128)} %copy.62), calls=%async_computation.5 | async-start | bytes 4194304 | tf_op jit(solution)/shard_map/all_to_all | solution.py:163
  552.5 2.2 copy-start.3
  561.6 44.0 %copy-start.1 = (bf16[128,256]{1,0:T(8,128)(2,1)S(1)}, bf16[128,256]{1,0:T(8,128)(2,1)}, u32[]{:S(2)}) copy-start(bf16[128,256]{1,0:T(8,128)(2,1)} %param.7) | copy-start | bytes 196612
  562.9 17.8 %all-to-all-start.7 = ((bf16[64,16,128]{2,1,0:T(8,128)(2,1)}), bf16[64,16,128]{2,1,0:T(8,128)(2,1)S(1)}, u32[]{:S(2)}, u32[]{:S(2)}) async-start(bf16[64,16,128]{2,1,0:T(8,128)(2,1)} %copy.70), calls=%async_computation.7 | async-start | bytes 524288 | tf_op jit(solution)/shard_map/all_to_all | solution.py:171
  580.7 23.4 %all-to-all-start.8 = ((f32[64,16,128]{2,1,0:T(8,128)}), f32[64,16,128]{2,1,0:T(8,128)S(1)}, u32[]{:S(2)}, u32[]{:S(2)}) async-start(f32[64,16,128]{2,1,0:T(8,128)} %copy.71), calls=%async_computation.8 | async-start | bytes 1048576 | tf_op jit(solution)/shard_map/all_to_all | solution.py:173
Sparse Core Ops, SparseCore 0:
  331.4 71.7 all-reduce.3
